TPU v7x, 32 devices: a whole 2x2x4 slice. The times are simulated.
32 devices in a mesh: box: 4 (over z), slab: 8 (over y, x, core).
Axes of the slice: x: 2, y: 2, z: 4, core: 2. Of those that a mesh axis runs over, the one named last changes fastest.
Arguments:
- hidden_field: bfloat16 [4, 8, 64, 128, 128], P('box', None, 'slab'), may hold values from -6 to 6
- cone_grad: float32 [256, 128, 128], P(('box', 'slab')), may hold values from -6 to 6
- conv_weight: bfloat16 [8, 27], replicated, may hold values from -0.4375 to 0.4375
- box_lower: int32 [256], P(('box', 'slab')), may hold values from 0 to 3, as said below
- box_upper: int32 [256], P(('box', 'slab')), may hold values from 0 to 3, as said below
- plane_lower: int32 [256], P(('box', 'slab')), may hold values from 0 to 63, as said below
- plane_upper: int32 [256], P(('box', 'slab')), may hold values from 0 to 63, as said below
- weight_lower: int32 [256], P(('box', 'slab')), may hold values from 0 to 256
- weight_upper: int32 [256], P(('box', 'slab')), may hold values from 0 to 256, as said below
Outputs:
- hidden_grad: bfloat16 [4, 8, 64, 128, 128], P('box', None, 'slab')
- weight_grad: float32 [8, 27], replicated
Inputs may be any that keep to these rules, and one draw needn't show every extreme that they name: With g = l // 64 the group of plane l, box_lower[l] is g or g - 1 (never below 0). box_upper[l] = min(box_lower[l] + 1, 3). Each box b has one offset o_b, and for one box, drawn from the seed, o_b = 32; plane_lower[l] = (l + o_b) mod 64 with b = box_lower[l]. plane_upper[l] = (l + o_b) mod 64 with b = box_upper[l], the same offsets. weight_upper[l] = 256 - weight_lower[l].
All inputs are finite; a program needn't handle non-finite values.
Results may differ from a plain program's by a relative error of at most 0.005.
Values may be sent and summed in bfloat16 or wider, within the bound.
A program may use at most 320 MiB of HBM per device.

v0:
```python
import math
import jax
import jax.numpy as jnp
from jax import lax
from jax.sharding import PartitionSpec as P

WDEN = 256


def passed_along(value, axis, steps):
    count = lax.axis_size(axis)
    first, last = (max(0, -steps), min(count, count - steps))
    return lax.ppermute(value, axis, [(source, source + steps) for source in range(first, last)])


def with_halo(cells, sides, width):
    for axis, dim in sides:
        count = lax.axis_size(axis)
        head = lax.slice_in_dim(cells, 0, width, axis=dim)
        tail = lax.slice_in_dim(cells, cells.shape[dim] - width, cells.shape[dim], axis=dim)
        cells = jnp.concatenate(
            [
                lax.ppermute(tail, axis, [(i, (i + 1) % count) for i in range(count)]),
                cells,
                lax.ppermute(head, axis, [((i + 1) % count, i) for i in range(count)]),
            ],
            axis=dim,
        )
    return cells


def wrap_sides(field):
    field = jnp.concatenate([field[:, -1:], field, field[:, :1]], 1)
    return jnp.concatenate([field[:, :, -1:], field, field[:, :, :1]], 2)


def local(
    hidden_field,
    cone_grad,
    conv_weight,
    box_lower,
    box_upper,
    plane_lower,
    plane_upper,
    weight_lower,
    weight_upper,
):
    group = lax.axis_index("box")
    column = lax.axis_index("slab")
    slab_count = lax.axis_size("slab")
    depth = cone_grad.shape[0]
    total_planes = depth * slab_count
    lower = weight_lower.astype(jnp.float32) / WDEN
    upper = weight_upper.astype(jnp.float32) / WDEN
    own_coef = jnp.where(box_lower == group, lower, 0.0) + jnp.where(box_upper == group, upper, 0.0)
    below_coef = jnp.where(box_lower == group - 1, lower, 0.0)
    above_coef = jnp.where(box_upper == group + 1, upper, 0.0)
    for_below = below_coef[:, None, None] * cone_grad
    for_above = above_coef[:, None, None] * cone_grad
    from_above = passed_along(for_below, "box", -1)
    from_below = passed_along(for_above, "box", 1)
    merged = (own_coef[:, None, None] * cone_grad + from_above + from_below).astype(jnp.bfloat16)
    first_plane = jnp.where(box_lower[0] == group, plane_lower[0], plane_upper[0])
    offset = (first_plane - column * depth) % total_planes
    whole = lax.all_gather(merged, "slab", axis=0, tiled=True)
    wanted = (column * depth + jnp.arange(depth, dtype=jnp.int32) - offset) % total_planes
    field_low = jnp.take(whole, wanted, axis=0)
    padded = with_halo(field_low, (("slab", 0),), 1)
    padded = wrap_sides(padded)[None, None]
    channel_count = hidden_field.shape[1]
    kernel = conv_weight.reshape(channel_count, 1, 3, 3, 3)[:, :, ::-1, ::-1, ::-1]
    numbers = ("NCDHW", "OIDHW", "NCDHW")
    hidden_grad = lax.conv_general_dilated(
        padded,
        kernel,
        (1, 1, 1),
        "VALID",
        dimension_numbers=numbers,
        preferred_element_type=jnp.float32,
    )
    hidden_grad = hidden_grad.astype(jnp.bfloat16).reshape(hidden_field.shape)
    as_kernel = hidden_field.reshape(
        channel_count, 1, depth, hidden_field.shape[3], hidden_field.shape[4]
    )
    partial_value = lax.conv_general_dilated(
        padded,
        as_kernel,
        (1, 1, 1),
        "VALID",
        dimension_numbers=numbers,
        preferred_element_type=jnp.float32,
    )
    partial_value = partial_value[0][:, ::-1, ::-1, ::-1].reshape(channel_count, 27)
    total = lax.psum(partial_value, ("box", "slab"))
    cells = lax.axis_size("box") * total_planes * field_low.shape[1] * field_low.shape[2]
    weight_grad = total * (1.0 / math.sqrt(cells))
    return (hidden_grad, weight_grad)


def solution(mesh):
    in_specs = (
        P("box", None, "slab", None, None),
        P(("box", "slab"), None, None),
        P(),
        P(("box", "slab")),
        P(("box", "slab")),
        P(("box", "slab")),
        P(("box", "slab")),
        P(("box", "slab")),
        P(("box", "slab")),
    )
    out_specs = (P("box", None, "slab", None, None), P())
    return jax.shard_map(local, mesh=mesh, in_specs=in_specs, out_specs=out_specs, check_vma=False)
```

profile of v0, /device:TPU:0, one launch (start us, length us, event | category | flops | bytes accessed | tf_op | source)
XLA Modules:
  0.0 805.5 jit_solution(18228177344446519526)
XLA Ops:
  7.2 0.7 fusion.3
  8.0 1.2 broadcast_multiply_fusion.1
  9.2 1.4 collective-permute-start
  10.6 5.6 collective-permute-start.1
  16.2 10.0 %collective-permute-done = f32[8,128,128]{2,1,0:T(8,128)S(1)} collective-permute-done((f32[8,128,128]{2,1,0:T(8,128)S(1)}, f32[8,128,128]{2,1,0:T(8,128)S(1)}, u32[]{:S(2)}, u32[]{:S(2)}) %collective-permute-start) | collective-permute-done | bytes 524320 | tf_op jit(solution)/shard_map/ppermute | solution.py:13
  26.1 1.2 collective-permute-done.1
  27.3 1.9 add_convert_fusion
  29.4 30.2 %all-gather.2.cloned.1.call-done = bf16[64,128,128]{2,1,0:T(8,128)(2,1)} async-done(((bf16[8,128,128]{2,1,0:T(8,128)(2,1)}), bf16[64,128,128]{2,1,0:T(8,128)(2,1)}) %all-gather.2.cloned.1.call-update) | async-done | bytes 2097168 | tf_op jit(solution)/shard_map/all_gather | solution.py:65
  59.6 2.2 gather_fusion
  61.9 0.3 collective-permute-start.2
  62.3 2.4 collective-permute-start.3
  64.6 69.5 %copy.41 = bf16[8,1,8,128,128]{0,1,4,3,2:T(2,128)(2,1)} copy(bf16[8,1,8,128,128]{4,3,2,0,1:T(8,128)(2,1)S(1)} %bitcast.34) | data formatting | bytes 4194304 | tf_op jit(solution)/shard_map/reshape | solution.py:82
  134.2 0.6 reshape.96
  135.0 0.2 fusion.7
  135.2 0.7 copy-done.2
  135.9 0.1 copy-done.4
  136.0 0.6 fusion.15
  136.6 184.9 %copy.40 = bf16[1,1,10,130,130]{1,0,4,3,2:T(2,128)(2,1)} copy(bf16[1,1,10,130,130]{4,3,2,1,0:T(8,128)(2,1)S(1)} %fusion.15) | data formatting | bytes 676000 | tf_op jit(solution)/shard_map/broadcast_in_dim | solution.py:69
  321.6 253.9 %fusion.9 = f32[1,8,3,3,3]{1,0,4,3,2:T(1,128)S(1)} fusion(bf16[1,1,10,130,130]{1,0,4,3,2:T(2,128)(2,1)} %copy.40, bf16[8,1,8,128,128]{0,1,4,3,2:T(2,128)(2,1)} %copy.41), kind=kOutput, calls=%fused_computation.40 | convolution fusion | flops 56623104 | bytes 2436016 | tf_op jit(solution)/shard_map/conv_general_dilated | solution.py:85
  575.5 39.6 %psum.7 = f32[8,27]{0,1:T(8,128)S(1)} all-reduce(f32[8,27]{0,1:T(8,128)S(1)} %reshape.75), channel_id=1, replica_groups=mesh['box'=4,'slab'=8] {'box','slab'}, use_global_device_ids=true, to_apply=%region_0.1 | all-reduce | flops 216 | bytes 1728 | tf_op jit(solution)/shard_map/psum | solution.py:94
  615.2 0.7 copy.43
  615.9 1.3 fusion.16
  617.1 0.4 copy.47
  617.5 0.1 pad.clone
  617.6 0.3 reshape.78
  618.0 0.4 fusion.2
  618.3 33.7 %copy.37 = bf16[1,10,130,8,19]{3,0,4,2,1:T(2,128)(2,1)} copy(bf16[1,10,130,8,19]{2,4,3,1,0:T(8,128)(2,1)S(1)} %fusion.2) | data formatting | bytes 790400 | tf_op jit(solution)/shard_map/conv_general_dilated | solution.py:73
  652.0 112.6 %fusion.10 = bf16[8,128,8,17,8]{4,2,3,1,0:T(8,128)(2,1)} fusion(bf16[1,10,130,8,19]{3,0,4,2,1:T(2,128)(2,1)} %copy.37, bf16[8,1,3,3,3]{0,1,4,3,2:T(2,128)(2,1)S(1)} %copy-done.13), kind=kOutput, calls=%fused_computation.41 | convolution fusion | flops 60162048 | bytes 2623856 | tf_op jit(solution)/shard_map/conv_general_dilated | solution.py:73
  764.6 30.5 %copy.39 = bf16[8,128,8,17,8]{1,4,3,2,0:T(8,128)(2,1)S(1)} copy(bf16[8,128,8,17,8]{4,2,3,1,0:T(8,128)(2,1)} %fusion.10) | data formatting | bytes 4456448 | tf_op jit(solution)/shard_map/conv_general_dilated | solution.py:73
  795.1 0.5 select_convert_fusion
  795.7 0.1 slice_bitcast_fusion
  795.8 2.9 copy.42
  (53 shorter events, 0.6 us)
Async XLA Ops:
  7.2 22.1 %copy-start.16 = (s32[8]{0:T(128)S(1)}, s32[8]{0:T(128)}, u32[]{:S(2)}) copy-start(s32[8]{0:T(128)} %param.12) | copy-start | bytes 100
  7.2 22.1 %copy-start.17 = (s32[8]{0:T(128)S(1)}, s32[8]{0:T(128)}, u32[]{:S(2)}) copy-start(s32[8]{0:T(128)} %param.14) | copy-start | bytes 100
  7.2 22.1 %copy-start.18 = (s32[8]{0:T(128)S(1)}, s32[8]{0:T(128)}, u32[]{:S(2)}) copy-start(s32[8]{0:T(128)} %param.15) | copy-start | bytes 100
  7.2 52.4 %all-gather.2.cloned.1.call-start = ((), (), s32[]{:S(2)}) async-start(), calls=%async_computation | async-start | bytes 2359296 | tf_op jit(solution)/shard_map/all_gather | solution.py:65
  9.1 55.5 %copy-start.6 = (bf16[1,8,8,128,128]{4,3,2,1,0:T(8,128)(2,1)S(1)}, bf16[1,8,8,128,128]{4,3,2,1,0:T(8,128)(2,1)}, u32[]{:S(2)}) copy-start(bf16[1,8,8,128,128]{4,3,2,1,0:T(8,128)(2,1)} %param.9) | copy-start | bytes 6291460
  9.2 17.0 %collective-permute-start = (f32[8,128,128]{2,1,0:T(8,128)S(1)}, f32[8,128,128]{2,1,0:T(8,128)S(1)}, u32[]{:S(2)}, u32[]{:S(2)}) collective-permute-start(f32[8,128,128]{2,1,0:T(8,128)S(1)} %get-tuple-element.8), channel_id=1, source_target_pairs={{8,0},{16,8},{24,16},{9,1},{17,9},{25,17},{10,2},{18,10},{26,18},{... | collective-permute-start | bytes 1572872 | tf_op jit(solution)/shard_map/ppermute | solution.py:13
  10.6 16.7 %collective-permute-start.1 = (f32[8,128,128]{2,1,0:T(8,128)S(1)}, f32[8,128,128]{2,1,0:T(8,128)S(1)}, u32[]{:S(2)}, u32[]{:S(2)}) collective-permute-start(f32[8,128,128]{2,1,0:T(8,128)S(1)} %get-tuple-element.9), channel_id=1, source_target_pairs={{0,8},{8,16},{16,24},{1,9},{9,17},{17,25},{2,10},{10,18},{18,26},{... | collective-permute-start | bytes 1572872 | tf_op jit(solution)/shard_map/ppermute | solution.py:13
  61.9 73.3 %copy-start = (bf16[8,128,128]{2,1,0:T(8,128)(2,1)}, bf16[8,128,128]{2,1,0:T(8,128)(2,1)S(1)}, u32[]{:S(2)}) copy-start(bf16[8,128,128]{2,1,0:T(8,128)(2,1)S(1)} %broadcast_select_fusion) | copy-start | bytes 786436
  61.9 72.9 %collective-permute-start.2 = (bf16[1,128,128]{2,1,0:T(8,128)(2,1)S(1)}, bf16[1,128,128]{2,1,0:T(8,128)(2,1)S(1)}, u32[]{:S(2)}, u32[]{:S(2)}) collective-permute-start(bf16[1,128,128]{2,1,0:T(8,128)(2,1)S(1)} %get-tuple-element.14), channel_id=1, source_target_pairs={{0,1},{1,2},{2,3},{3,4},{4,5},{5,6},{6,7},{7,0},{8,9},{9,10},{10,1... | collective-permute-start | bytes 98312 | tf_op jit(solution)/shard_map/ppermute | solution.py:23
  62.3 72.6 %collective-permute-start.3 = (bf16[1,128,128]{2,1,0:T(8,128)(2,1)S(1)}, bf16[1,128,128]{2,1,0:T(8,128)(2,1)S(1)}, u32[]{:S(2)}, u32[]{:S(2)}) collective-permute-start(bf16[1,128,128]{2,1,0:T(8,128)(2,1)S(1)} %get-tuple-element.15), channel_id=1, source_target_pairs={{1,0},{2,1},{3,2},{4,3},{5,4},{6,5},{7,6},{0,7},{9,8},{10,9},{11,1... | collective-permute-start | bytes 98312 | tf_op jit(solution)/shard_map/ppermute | solution.py:25
  64.6 69.5 %copy-start.14 = (bf16[8,27]{1,0:T(8,128)(2,1)S(1)}, bf16[8,27]{1,0:T(8,128)(2,1)}, u32[]{:S(2)}) copy-start(bf16[8,27]{1,0:T(8,128)(2,1)} %param.11) | copy-start | bytes 1300
  134.9 1.8 copy-start.7
  134.9 1.8 copy-start.9
  134.9 186.7 %copy-start.11 = (bf16[10,1,128]{2,1,0:T(2,128)(2,1)}, bf16[10,1,128]{2,1,0:T(2,128)(2,1)S(1)}, u32[]{:S(2)}) copy-start(bf16[10,1,128]{2,1,0:T(2,128)(2,1)S(1)} %get-tuple-element.12) | copy-start | bytes 7684
  134.9 186.6 %copy-start.12 = (bf16[10,1,128]{2,1,0:T(2,128)(2,1)}, bf16[10,1,128]{2,1,0:T(2,128)(2,1)S(1)}, u32[]{:S(2)}) copy-start(bf16[10,1,128]{2,1,0:T(2,128)(2,1)S(1)} %get-tuple-element.13) | copy-start | bytes 7684
  135.2 0.7 copy-start.2
  135.2 0.8 copy-start.4
  321.6 294.3 %copy-start.1 = (bf16[8,128,128]{2,1,0:T(8,128)(2,1)S(1)}, bf16[8,128,128]{2,1,0:T(8,128)(2,1)}, u32[]{:S(2)}) copy-start(bf16[8,128,128]{2,1,0:T(8,128)(2,1)} %copy-done) | copy-start | bytes 786436
  321.6 294.3 %copy-start.3 = (bf16[10,130,1]{2,1,0:T(8,128)(2,1)S(1)}, bf16[10,130,1]{2,1,0:T(8,128)(2,1)}, u32[]{:S(2)}) copy-start(bf16[10,130,1]{2,1,0:T(8,128)(2,1)} %copy-done.2) | copy-start | bytes 7804
  321.6 294.3 %copy-start.5 = (bf16[10,130,1]{2,1,0:T(8,128)(2,1)S(1)}, bf16[10,130,1]{2,1,0:T(8,128)(2,1)}, u32[]{:S(2)}) copy-start(bf16[10,130,1]{2,1,0:T(8,128)(2,1)} %copy-done.4) | copy-start | bytes 7804
  321.6 294.3 %copy-start.8 = (bf16[1,128,128]{2,1,0:T(8,128)(2,1)S(1)}, bf16[1,128,128]{2,1,0:T(8,128)(2,1)}, u32[]{:S(2)}) copy-start(bf16[1,128,128]{2,1,0:T(8,128)(2,1)} %copy-done.7) | copy-start | bytes 98308
  321.6 294.3 %copy-start.10 = (bf16[1,128,128]{2,1,0:T(8,128)(2,1)S(1)}, bf16[1,128,128]{2,1,0:T(8,128)(2,1)}, u32[]{:S(2)}) copy-start(bf16[1,128,128]{2,1,0:T(8,128)(2,1)} %copy-done.9) | copy-start | bytes 98308
  618.3 33.7 %copy-start.13 = (bf16[8,1,3,3,3]{0,1,4,3,2:T(2,128)(2,1)S(1)}, bf16[8,1,3,3,3]{0,1,4,3,2:T(2,128)(2,1)}, u32[]{:S(2)}) copy-start(bf16[8,1,3,3,3]{0,1,4,3,2:T(2,128)(2,1)} %reshape.96) | copy-start | bytes 1300
  764.6 30.5 %copy-start.15 = (pred[8,17]{1,0:T(8,128)(4,1)S(1)}, pred[8,17]{1,0:T(8,128)(4,1)}, u32[]{:S(2)}) copy-start(pred[8,17]{1,0:T(8,128)(4,1)} %constant.70) | copy-start | bytes 412
Sparse Core Ops, SparseCore 0:
  29.3 30.2 all-gather.1
where the time goes:
time: 806 us
  matrix products  366 us (45%)
  local copies, waits for them, and re-layouts  327 us (41%)
  waiting for transfers between devices  41.4 us (5%)
  blocking collectives  39.6 us (5%)
  between operations  14.5 us (2%)
  starting transfers between devices  9.75 us (1%)
    conv_general_dilated x1, matrix products, local(): lax.conv_general_dilated(padded, as_kernel, (1, 1, 1), 'VALID', dimension...  254 us
    broadcast_in_dim x2, local copies, waits for them, and re-layouts, local(): padded = wrap_sides(padded)[None, None]  185 us
    conv_general_dilated x1, matrix products, local(): lax.conv_general_dilated(padded, kernel, (1, 1, 1), 'VALID', dimension_nu...  113 us
    reshape x1, local copies, waits for them, and re-layouts, local(): hidden_field.reshape(channel_count, 1, depth, hidden_field.shape[3], hidd...  69.5 us
    conv_general_dilated x4, local copies, waits for them, and re-layouts, local(): lax.conv_general_dilated(padded, kernel, (1, 1, 1), 'VALID', dimension_nu...  64.5 us
    psum x1, blocking collectives, local(): total = lax.psum(partial_value, ('box', 'slab'))  39.6 us
    all_gather x1, waiting for transfers between devices, local(): whole = lax.all_gather(merged, 'slab', axis=0, tiled=True)  30.2 us
  transfers between devices with their start and end apart: 5, of which 3 were waited for; matrix products, arithmetic and copies ran while one was open for 9% of the time, Pallas kernels for 0%

commit v1 on v0

--- a/solution.py
+++ b/solution.py
@@ -5,6 +5,17 @@
 from jax.sharding import PartitionSpec as P
 
 WDEN = 256
+
+
+def ring_gather(array, axis, dim):
+    ways = lax.axis_size(axis)
+    pieces = [array]
+    for far in range(1, ways):
+        pieces.append(
+            lax.ppermute(pieces[far - 1], axis, [(d, (d - 1) % ways) for d in range(ways)])
+        )
+    line = jnp.concatenate(pieces, axis=dim)
+    return jnp.roll(line, lax.axis_index(axis) * array.shape[dim], axis=dim)
 
 
 def passed_along(value, axis, steps):
@@ -62,7 +73,7 @@
     merged = (own_coef[:, None, None] * cone_grad + from_above + from_below).astype(jnp.bfloat16)
     first_plane = jnp.where(box_lower[0] == group, plane_lower[0], plane_upper[0])
     offset = (first_plane - column * depth) % total_planes
-    whole = lax.all_gather(merged, "slab", axis=0, tiled=True)
+    whole = ring_gather(merged, "slab", 0)
     wanted = (column * depth + jnp.arange(depth, dtype=jnp.int32) - offset) % total_planes
     field_low = jnp.take(whole, wanted, axis=0)
     padded = with_halo(field_low, (("slab", 0),), 1)

time: 806 us -> 841 us (1.043); the launches traced: 806 us -> 832 us
  local copies, waits for them, and re-layouts: 327 us -> 355 us
  starting transfers between devices: 9.75 us -> 27.4 us
  between operations: 14.5 us -> 2.91 us
  waiting for transfers between devices: 41.4 us -> 32 us
    all_gather x1 -> x0, waiting for transfers between devices: 30.2 us -> none  [local(): whole = lax.all_gather(merged, 'slab', axis=0, tiled=True)]
    ppermute x0 -> x7, waiting for transfers between devices: none -> 20.8 us  [ring_gather(): lax.ppermute(pieces[far - 1], axis, [(d, (d - 1) % ways) for d in range(w...]
    ppermute x0 -> x7, starting transfers between devices: none -> 17.7 us  [ring_gather(): lax.ppermute(pieces[far - 1], axis, [(d, (d - 1) % ways) for d in range(w...]
    reshape x1, local copies, waits for them, and re-layouts: 69.5 us -> 86.2 us  [local(): hidden_field.reshape(channel_count, 1, depth, hidden_field.shape[3], hidd...]
    unnamed x43 -> x49, local copies, waits for them, and re-layouts: 4.93 us -> 15 us
  transfers between devices with their start and end apart: 5 -> 11, of which waited for: 3 -> 9; matrix products, arithmetic and copies ran while one was open for 9% -> 11% of each run, Pallas kernels for 0% -> 0%
where the time goes in v1:
time: 841 us; the launch traced here: 832 us
  matrix products  367 us (44%)
  local copies, waits for them, and re-layouts  355 us (42%)
  blocking collectives  40.9 us (5%)
  waiting for transfers between devices  32 us (4%)
  starting transfers between devices  27.4 us (3%)
    conv_general_dilated x1, matrix products, local(): lax.conv_general_dilated(padded, as_kernel, (1, 1, 1), 'VALID', dimension...  254 us
    broadcast_in_dim x2, local copies, waits for them, and re-layouts, local(): padded = wrap_sides(padded)[None, None]  185 us
    conv_general_dilated x1, matrix products, local(): lax.conv_general_dilated(padded, kernel, (1, 1, 1), 'VALID', dimension_nu...  113 us
    reshape x1, local copies, waits for them, and re-layouts, local(): hidden_field.reshape(channel_count, 1, depth, hidden_field.shape[3], hidd...  86.2 us
    conv_general_dilated x4, local copies, waits for them, and re-layouts, local(): lax.conv_general_dilated(padded, kernel, (1, 1, 1), 'VALID', dimension_nu...  64.7 us
    psum x1, blocking collectives, local(): total = lax.psum(partial_value, ('box', 'slab'))  40.9 us
    ppermute x7, waiting for transfers between devices, ring_gather(): lax.ppermute(pieces[far - 1], axis, [(d, (d - 1) % ways) for d in range(w...  20.8 us
    ppermute x7, starting transfers between devices, ring_gather(): lax.ppermute(pieces[far - 1], axis, [(d, (d - 1) % ways) for d in range(w...  17.7 us
  transfers between devices with their start and end apart: 11, of which 9 were waited for; matrix products, arithmetic and copies ran while one was open for 11% of the time, Pallas kernels for 0%

profile of v1, /device:TPU:0, one launch (start us, length us, event | category | flops | bytes accessed | tf_op | source)
XLA Modules:
  0.0 831.7 jit_solution(82397799062177478)
XLA Ops:
  1.4 1.2 broadcast_multiply_fusion.1
  2.5 1.3 collective-permute-start
  3.8 5.6 collective-permute-start.1
  9.4 10.0 %collective-permute-done = f32[8,128,128]{2,1,0:T(8,128)S(1)} collective-permute-done((f32[8,128,128]{2,1,0:T(8,128)S(1)}, f32[8,128,128]{2,1,0:T(8,128)S(1)}, u32[]{:S(2)}, u32[]{:S(2)}) %collective-permute-start) | collective-permute-done | bytes 524320 | tf_op jit(solution)/shard_map/ppermute | solution.py:24
  19.4 1.2 collective-permute-done.1
  20.6 1.9 constant_dynamic-update-slice_fusion.15
  22.5 0.9 collective-permute-start.2
  23.3 3.9 collective-permute-done.2
  27.2 2.8 collective-permute-start.3
  30.0 3.9 collective-permute-done.3
  33.9 2.8 collective-permute-start.4
  36.7 3.9 collective-permute-done.4
  40.6 2.8 collective-permute-start.5
  45.4 1.9 collective-permute-done.5
  47.3 2.8 collective-permute-start.6
  50.2 3.8 collective-permute-done.6
  54.0 2.8 collective-permute-start.7
  59.0 1.7 collective-permute-done.7
  60.7 2.8 collective-permute-start.8
  65.0 0.7 constant_dynamic-update-slice_fusion.9
  65.7 1.7 collective-permute-done.8
  73.9 1.7 constant_dynamic-slice_fusion
  76.3 2.9 collective-permute-start.10
  79.2 86.2 %copy.31 = bf16[8,1,8,128,128]{0,1,4,3,2:T(2,128)(2,1)} copy(bf16[8,1,8,128,128]{4,3,2,0,1:T(8,128)(2,1)} %bitcast.34) | data formatting | bytes 4194304 | tf_op jit(solution)/shard_map/reshape | solution.py:93
  167.9 185.0 %copy.30 = bf16[1,1,10,130,130]{1,0,4,3,2:T(2,128)(2,1)} copy(bf16[1,1,10,130,130]{4,3,2,1,0:T(8,128)(2,1)S(1)} %fusion.15) | data formatting | bytes 676000 | tf_op jit(solution)/shard_map/broadcast_in_dim | solution.py:80
  352.9 254.1 %fusion.9 = f32[1,8,3,3,3]{1,0,4,3,2:T(1,128)S(1)} fusion(bf16[1,1,10,130,130]{1,0,4,3,2:T(2,128)(2,1)} %copy.30, bf16[8,1,8,128,128]{0,1,4,3,2:T(2,128)(2,1)} %copy.31), kind=kOutput, calls=%fused_computation.57 | convolution fusion | flops 56623104 | bytes 2436016 | tf_op jit(solution)/shard_map/conv_general_dilated | solution.py:96
  607.0 40.9 %psum.7 = f32[8,27]{0,1:T(8,128)S(1)} all-reduce(f32[8,27]{0,1:T(8,128)S(1)} %reshape.75), channel_id=1, replica_groups=mesh['box'=4,'slab'=8] {'box','slab'}, use_global_device_ids=true, to_apply=%region_0.1 | all-reduce | flops 216 | bytes 1728 | tf_op jit(solution)/shard_map/psum | solution.py:105
  648.6 1.3 fusion.16
  651.2 33.9 %copy.27 = bf16[1,10,130,8,19]{3,0,4,2,1:T(2,128)(2,1)} copy(bf16[1,10,130,8,19]{2,4,3,1,0:T(8,128)(2,1)S(1)} %fusion.2) | data formatting | bytes 790400 | tf_op jit(solution)/shard_map/conv_general_dilated | solution.py:84
  685.1 112.6 %fusion.10 = bf16[8,128,8,17,8]{4,2,3,1,0:T(8,128)(2,1)} fusion(bf16[1,10,130,8,19]{3,0,4,2,1:T(2,128)(2,1)} %copy.27, bf16[8,1,3,3,3]{0,1,4,3,2:T(2,128)(2,1)S(1)} %copy-done.12), kind=kOutput, calls=%fused_computation.58 | convolution fusion | flops 60162048 | bytes 2623856 | tf_op jit(solution)/shard_map/conv_general_dilated | solution.py:84
  797.7 30.5 %copy.29 = bf16[8,128,8,17,8]{1,4,3,2,0:T(8,128)(2,1)S(1)} copy(bf16[8,128,8,17,8]{4,2,3,1,0:T(8,128)(2,1)} %fusion.10) | data formatting | bytes 4456448 | tf_op jit(solution)/shard_map/conv_general_dilated | solution.py:84
  828.9 2.9 copy.32
  (72 shorter events, 16.6 us)
Async XLA Ops:
  2.5 16.8 %collective-permute-start = (f32[8,128,128]{2,1,0:T(8,128)S(1)}, f32[8,128,128]{2,1,0:T(8,128)S(1)}, u32[]{:S(2)}, u32[]{:S(2)}) collective-permute-start(f32[8,128,128]{2,1,0:T(8,128)S(1)} %get-tuple-element.8), channel_id=1, source_target_pairs={{8,0},{16,8},{24,16},{9,1},{17,9},{25,17},{10,2},{18,10},{26,18},{... | collective-permute-start | bytes 1572872 | tf_op jit(solution)/shard_map/ppermute | solution.py:24
  3.8 16.7 %collective-permute-start.1 = (f32[8,128,128]{2,1,0:T(8,128)S(1)}, f32[8,128,128]{2,1,0:T(8,128)S(1)}, u32[]{:S(2)}, u32[]{:S(2)}) collective-permute-start(f32[8,128,128]{2,1,0:T(8,128)S(1)} %get-tuple-element.9), channel_id=1, source_target_pairs={{0,8},{8,16},{16,24},{1,9},{9,17},{17,25},{2,10},{10,18},{18,26},{... | collective-permute-start | bytes 1572872 | tf_op jit(solution)/shard_map/ppermute | solution.py:24
  22.5 4.7 collective-permute-start.2
  27.2 6.7 collective-permute-start.3
  33.9 6.7 collective-permute-start.4
  40.6 6.7 collective-permute-start.5
  47.3 6.7 collective-permute-start.6
  54.0 6.7 collective-permute-start.7
  60.7 6.7 collective-permute-start.8
  76.3 90.2 %copy-start = (bf16[8,128,128]{2,1,0:T(8,128)(2,1)}, bf16[8,128,128]{2,1,0:T(8,128)(2,1)S(1)}, u32[]{:S(2)}) copy-start(bf16[8,128,128]{2,1,0:T(8,128)(2,1)S(1)} %broadcast_select_fusion) | copy-start | bytes 786436
  76.3 89.8 %collective-permute-start.10 = (bf16[1,128,128]{2,1,0:T(8,128)(2,1)S(1)}, bf16[1,128,128]{2,1,0:T(8,128)(2,1)S(1)}, u32[]{:S(2)}, u32[]{:S(2)}) collective-permute-start(bf16[1,128,128]{2,1,0:T(8,128)(2,1)S(1)} %get-tuple-element.15), channel_id=1, source_target_pairs={{1,0},{2,1},{3,2},{4,3},{5,4},{6,5},{7,6},{0,7},{9,8},{10,9},{11,1... | collective-permute-start | bytes 98312 | tf_op jit(solution)/shard_map/ppermute | solution.py:36
  79.2 86.9 %collective-permute-start.9 = (bf16[1,128,128]{2,1,0:T(8,128)(2,1)S(1)}, bf16[1,128,128]{2,1,0:T(8,128)(2,1)S(1)}, u32[]{:S(2)}, u32[]{:S(2)}) collective-permute-start(bf16[1,128,128]{2,1,0:T(8,128)(2,1)S(1)} %get-tuple-element.14), channel_id=1, source_target_pairs={{0,1},{1,2},{2,3},{3,4},{4,5},{5,6},{6,7},{7,0},{8,9},{9,10},{10,1... | collective-permute-start | bytes 98312 | tf_op jit(solution)/shard_map/ppermute | solution.py:34
  79.2 86.2 %copy-start.13 = (bf16[8,27]{1,0:T(8,128)(2,1)S(1)}, bf16[8,27]{1,0:T(8,128)(2,1)}, u32[]{:S(2)}) copy-start(bf16[8,27]{1,0:T(8,128)(2,1)} %param.11) | copy-start | bytes 1300
  166.1 186.8 %copy-start.6 = (bf16[1,128,128]{2,1,0:T(8,128)(2,1)}, bf16[1,128,128]{2,1,0:T(8,128)(2,1)S(1)}, u32[]{:S(2)}) copy-start(bf16[1,128,128]{2,1,0:T(8,128)(2,1)S(1)} %collective-permute-done.10) | copy-start | bytes 98308
  166.1 186.7 %copy-start.7 = (bf16[1,128,128]{2,1,0:T(8,128)(2,1)}, bf16[1,128,128]{2,1,0:T(8,128)(2,1)S(1)}, u32[]{:S(2)}) copy-start(bf16[1,128,128]{2,1,0:T(8,128)(2,1)S(1)} %collective-permute-done.9) | copy-start | bytes 98308
  166.2 0.6 copy-start.8
  166.2 0.6 copy-start.10
  166.5 0.7 copy-start.2
  166.5 0.8 copy-start.4
  352.9 295.7 %copy-start.1 = (bf16[8,128,128]{2,1,0:T(8,128)(2,1)S(1)}, bf16[8,128,128]{2,1,0:T(8,128)(2,1)}, u32[]{:S(2)}) copy-start(bf16[8,128,128]{2,1,0:T(8,128)(2,1)} %copy-done) | copy-start | bytes 786436
  352.9 295.7 %copy-start.3 = (bf16[10,130,1]{2,1,0:T(8,128)(2,1)S(1)}, bf16[10,130,1]{2,1,0:T(8,128)(2,1)}, u32[]{:S(2)}) copy-start(bf16[10,130,1]{2,1,0:T(8,128)(2,1)} %copy-done.2) | copy-start | bytes 7804
  352.9 295.7 %copy-start.5 = (bf16[10,130,1]{2,1,0:T(8,128)(2,1)S(1)}, bf16[10,130,1]{2,1,0:T(8,128)(2,1)}, u32[]{:S(2)}) copy-start(bf16[10,130,1]{2,1,0:T(8,128)(2,1)} %copy-done.4) | copy-start | bytes 7804
  352.9 295.7 %copy-start.9 = (bf16[10,1,128]{2,1,0:T(2,128)(2,1)S(1)}, bf16[10,1,128]{2,1,0:T(2,128)(2,1)}, u32[]{:S(2)}) copy-start(bf16[10,1,128]{2,1,0:T(2,128)(2,1)} %copy-done.8) | copy-start | bytes 7684
  352.9 295.7 %copy-start.11 = (bf16[10,1,128]{2,1,0:T(2,128)(2,1)S(1)}, bf16[10,1,128]{2,1,0:T(2,128)(2,1)}, u32[]{:S(2)}) copy-start(bf16[10,1,128]{2,1,0:T(2,128)(2,1)} %copy-done.10) | copy-start | bytes 7684
  651.2 33.9 %copy-start.12 = (bf16[8,1,3,3,3]{0,1,4,3,2:T(2,128)(2,1)S(1)}, bf16[8,1,3,3,3]{0,1,4,3,2:T(2,128)(2,1)}, u32[]{:S(2)}) copy-start(bf16[8,1,3,3,3]{0,1,4,3,2:T(2,128)(2,1)} %reshape.96) | copy-start | bytes 1300
  797.7 30.5 %copy-start.14 = (pred[8,17]{1,0:T(8,128)(4,1)S(1)}, pred[8,17]{1,0:T(8,128)(4,1)}, u32[]{:S(2)}) copy-start(pred[8,17]{1,0:T(8,128)(4,1)} %constant.86) | copy-start | bytes 412
